TPU v7x, 32 devices: a whole 2x2x4 slice. The times are simulated.
32 devices in a mesh: stream: 16 (over z, y, core), span: 2 (over x).
Axes of the slice: x: 2, y: 2, z: 4, core: 2. Of those that a mesh axis runs over, the one named last changes fastest.
Arguments:
- basis: float32 [4, 10, 128, 8, 256], P(None, None, 'stream', None, 'span'), may hold values from -6 to 6
- coeffs: float32 [4], replicated, may hold values from -3 to 3
- mixing_matrix: float32 [10, 10], replicated, may hold values from -2 to 2
- base_speed: float32 [128, 8, 256], P('stream', None, 'span'), may hold values from 0.5 to 1.5
- span_speed: float32 [128, 8, 256], P('stream', None, 'span'), may hold values from -2.4 to 2.4
- polymer_gain: float32 [128, 8, 256], P('stream', None, 'span'), may hold values from 0.3 to 3
Outputs:
- proj: float32 [4, 4], replicated
- rfactor: float32 [4, 4], replicated
- basis_new: float32 [4, 10, 128, 8, 256], P(None, None, 'stream', None, 'span')
All inputs are finite; a program needn't handle non-finite values.
Results may differ from a plain program's by a relative error of at most 0.00025.
Values sent between devices are 32-bit elements; how exact they have to be, the bound alone decides.
A program may use at most 64 MiB of HBM per device.

v0:
```python
import jax
import jax.numpy as jnp
from jax import lax
from jax.sharding import PartitionSpec as P

STEPS = 4


def padded(value, sides, width):
    for axis, dim in sides:
        size, length = (lax.axis_size(axis), value.shape[dim])
        up = [(i, (i + 1) % size) for i in range(size)]
        down = [(j, i) for i, j in up]
        last = lax.slice_in_dim(value, length - width, length, axis=dim)
        leading = lax.slice_in_dim(value, 0, width, axis=dim)
        before = lax.ppermute(last, axis, up)
        after = lax.ppermute(leading, axis, down)
        value = jnp.concatenate([before, value, after], axis=dim)
    return value


def advance(values_now, base_speed, span_speed, polymer_gain, mixing_matrix):
    center_part = values_now[:, 1:-1, :, 1:-1]
    forward_x = values_now[:, 2:, :, 1:-1]
    backward_x = values_now[:, :-2, :, 1:-1]
    forward_z = values_now[:, 1:-1, :, 2:]
    backward_z = values_now[:, 1:-1, :, :-2]
    zero_row = jnp.zeros_like(center_part[:, :, :1, :])
    wall_up = jnp.concatenate([center_part[:, :, 1:, :], zero_row], axis=2)
    wall_down = jnp.concatenate([zero_row, center_part[:, :, :-1, :]], axis=2)
    laplace = (
        forward_x + backward_x + forward_z + backward_z + wall_up + wall_down - 6.0 * center_part
    )
    mixing = jnp.einsum(
        "fg,gxyz->fxyz", mixing_matrix, center_part, precision=lax.Precision.HIGHEST
    )
    return (
        -base_speed * (forward_x - backward_x) * 0.5
        - span_speed * (forward_z - backward_z) * 0.5
        + 0.05 * laplace
        + polymer_gain * mixing
    )


def on_device(basis, coeffs, mixing_matrix, base_speed, span_speed, polymer_gain):
    total = float(basis[0].size * lax.axis_size("stream") * lax.axis_size("span"))
    start = jnp.einsum("m,mfxyz->fxyz", coeffs, basis, precision=lax.Precision.HIGHEST)
    krylov = []
    current = start
    for section in range(STEPS):
        rimmed = padded(current, (("stream", 1), ("span", 3)), 1)
        current = advance(rimmed, base_speed, span_speed, polymer_gain, mixing_matrix)
        krylov.append(current)
    stacked = jnp.stack(krylov, 0)
    flat_basis = basis.reshape(basis.shape[0], -1)
    flat_new = stacked.reshape(STEPS, -1)
    local_proj = jnp.dot(flat_basis, flat_new.T, precision=lax.Precision.HIGHEST)
    proj = lax.psum(local_proj, ("stream", "span")) / total
    projected = flat_new - jnp.dot(proj.T, flat_basis, precision=lax.Precision.HIGHEST)
    local_gram = jnp.dot(projected, projected.T, precision=lax.Precision.HIGHEST)
    gram = lax.psum(local_gram, ("stream", "span")) / total
    lower_factor = jnp.linalg.cholesky(gram)
    solved = jax.scipy.linalg.solve_triangular(lower_factor, projected, lower=True)
    return (proj, lower_factor.T, solved.reshape(stacked.shape))


def solution(mesh):
    placed = (
        P(None, None, "stream", None, "span"),
        P(),
        P(),
        P("stream", None, "span"),
        P("stream", None, "span"),
        P("stream", None, "span"),
    )
    return jax.shard_map(
        on_device,
        mesh=mesh,
        in_specs=placed,
        out_specs=(P(), P(), P(None, None, "stream", None, "span")),
        check_vma=False,
    )
```

profile of v0, /device:TPU:0, one launch (start us, length us, event | category | flops | bytes accessed | tf_op | source)
XLA Modules:
  0.0 180.0 jit_solution(8099287838283555727)
XLA Ops:
  0.6 4.3 %fusion.12 = f32[1,10,8,8,128]{4,0,3,2,1:T(1,128)S(1)} fusion(f32[4,10,8,8,128]{4,3,2,1,0:T(8,128)} %param.6, f32[4]{0:T(128)} %param.7), kind=kOutput, calls=%fused_computation.18 | convolution fusion | flops 3932160 | bytes 1638416 | tf_op jit(solution)/shard_map/m,mfxyz->fxyz/dot_general | solution.py:47
  5.1 5.5 %collective-permute-start = (f32[10,1,8,128]{3,0,2,1:T(8,128)S(1)}, f32[10,1,8,128]{3,0,2,1:T(8,128)S(1)}, u32[]{:S(2)}, u32[]{:S(2)}) collective-permute-start(f32[10,1,8,128]{3,0,2,1:T(8,128)S(1)} %get-tuple-element.33), channel_id=1, source_target_pairs={{2,0},{4,2},{6,4},{8,6},{10,8},{12,10},{14,12},{16,14},{18,16},{20... | collective-permute-start | bytes 122888 | tf_op jit(solution)/shard_map/ppermute | solution.py:17
  10.6 1.9 %collective-permute-done = f32[10,1,8,128]{3,0,2,1:T(8,128)S(1)} collective-permute-done((f32[10,1,8,128]{3,0,2,1:T(8,128)S(1)}, f32[10,1,8,128]{3,0,2,1:T(8,128)S(1)}, u32[]{:S(2)}, u32[]{:S(2)}) %collective-permute-start) | collective-permute-done | bytes 40992 | tf_op jit(solution)/shard_map/ppermute | solution.py:17
  12.5 4.5 %collective-permute-done.1 = f32[10,1,8,128]{3,0,2,1:T(8,128)S(1)} collective-permute-done((f32[10,1,8,128]{3,0,2,1:T(8,128)S(1)}, f32[10,1,8,128]{3,0,2,1:T(8,128)S(1)}, u32[]{:S(2)}, u32[]{:S(2)}) %collective-permute-start.1) | collective-permute-done | bytes 40992 | tf_op jit(solution)/shard_map/ppermute | solution.py:16
  17.3 0.6 copy.31
  17.9 1.5 collective-permute-start.2
  19.5 0.6 copy.33
  20.1 0.6 collective-permute-start.3
  20.8 1.2 collective-permute-done.2
  22.0 1.0 copy.32
  23.0 1.2 collective-permute-done.3
  24.1 1.0 copy.34
  25.1 0.9 fusion.11
  26.1 0.5 collective-permute-start.5
  26.6 1.4 collective-permute-done.4
  28.0 4.5 %collective-permute-done.5 = f32[10,1,8,128]{3,0,2,1:T(8,128)S(1)} collective-permute-done((f32[10,1,8,128]{3,0,2,1:T(8,128)S(1)}, f32[10,1,8,128]{3,0,2,1:T(8,128)S(1)}, u32[]{:S(2)}, u32[]{:S(2)}) %collective-permute-start.5) | collective-permute-done | bytes 40992 | tf_op jit(solution)/shard_map/ppermute | solution.py:16
  32.9 0.6 copy.35
  33.5 0.6 collective-permute-start.6
  34.1 0.6 copy.37
  34.7 1.5 collective-permute-start.7
  36.3 1.3 collective-permute-done.6
  37.6 1.0 copy.36
  38.7 1.0 copy.38
  39.7 0.9 fusion.9
  40.7 0.5 collective-permute-start.9
  41.2 1.4 collective-permute-done.8
  42.6 4.7 %collective-permute-done.9 = f32[10,1,8,128]{3,0,2,1:T(8,128)S(1)} collective-permute-done((f32[10,1,8,128]{3,0,2,1:T(8,128)S(1)}, f32[10,1,8,128]{3,0,2,1:T(8,128)S(1)}, u32[]{:S(2)}, u32[]{:S(2)}) %collective-permute-start.9) | collective-permute-done | bytes 40992 | tf_op jit(solution)/shard_map/ppermute | solution.py:16
  47.6 0.6 copy.39
  48.2 1.5 collective-permute-start.10
  49.8 0.6 copy.41
  50.4 0.6 collective-permute-start.11
  51.0 0.8 fusion.36
  51.8 0.5 collective-permute-done.10
  52.3 1.0 copy.40
  53.3 1.2 collective-permute-done.11
  54.4 1.0 copy.42
  55.4 1.9 %fusion.7 = f32[10,8,8,128]{3,0,2,1:T(8,128)S(1)} fusion(f32[10,8,8,128]{3,0,2,1:T(8,128)S(1)} %fusion.9, f32[10,8,7,128]{3,0,2,1:T(8,128)} %get-tuple-element.27, f32[10,8,7,128]{3,0,2,1:T(8,128)S(1)} %get-tuple-element.26, f32[10,10,8,1]{3,0,2,1:T(8,128)S(1)} %copy.40, f32[10,1,8,128]{3,0,2,1:T(8,128)S(1)} %collective-permute-done.8, ...), kind=kOutput, calls=%fused_computation.11 | convolution fusion | flops 11960320 | bytes 1415824 | tf_op jit(solution)/shard_map/fg,gxyz->fxyz/dot_general | solution.py:34
  57.4 0.5 collective-permute-start.13
  57.9 0.8 copy.49
  58.8 0.8 copy.50
  59.6 4.3 %collective-permute-done.13 = f32[10,1,8,128]{3,0,2,1:T(8,128)S(1)} collective-permute-done((f32[10,1,8,128]{3,0,2,1:T(8,128)S(1)}, f32[10,1,8,128]{3,0,2,1:T(8,128)S(1)}, u32[]{:S(2)}, u32[]{:S(2)}) %collective-permute-start.13) | collective-permute-done | bytes 40992 | tf_op jit(solution)/shard_map/ppermute | solution.py:16
  64.2 0.6 copy.43
  64.8 0.6 collective-permute-start.14
  65.4 0.6 copy.45
  66.0 1.5 collective-permute-start.15
  67.5 0.8 fusion.34
  68.3 0.8 copy.51
  69.2 1.0 copy.44
  70.1 1.0 copy.46
  71.1 2.0 %fusion.5 = f32[10,8,8,128]{3,0,2,1:T(8,128)S(1)} fusion(f32[10,8,8,128]{3,0,2,1:T(8,128)S(1)} %fusion.7, f32[10,8,7,128]{3,0,2,1:T(8,128)} %get-tuple-element.23, f32[10,8,7,128]{3,0,2,1:T(8,128)S(1)} %get-tuple-element.22, f32[10,10,8,1]{3,0,2,1:T(8,128)S(1)} %copy.44, f32[10,1,8,128]{3,0,2,1:T(8,128)S(1)} %collective-permute-done.12, ...), kind=kOutput, calls=%fused_computation.8 | convolution fusion | flops 11960320 | bytes 1415824 | tf_op jit(solution)/shard_map/fg,gxyz->fxyz/dot_general | solution.py:34
  73.3 1.1 copy-done.1
  74.4 6.8 %fusion.15 = f32[4,4]{0,1:T(4,128)S(1)} fusion(f32[4,10,8,8,128]{4,3,2,1,0:T(8,128)S(1)} %copy-done.1, f32[4,10,8,8,128]{4,1,3,2,0:T(8,128)S(1)} %pad_maximum_fusion), kind=kOutput, calls=%fused_computation.21 | convolution fusion | flops 15728640 | bytes 2621504 | tf_op jit(solution)/shard_map/dot_general | solution.py:57
  81.2 0.8 copy.52
  82.0 37.1 %psum.14 = f32[4,4]{0,1:T(4,128)S(1)} all-reduce(f32[4,4]{0,1:T(4,128)S(1)} %fusion.15), channel_id=1, replica_groups=mesh['stream'=16,'span'=2] {'stream','span'}, use_global_device_ids=true, to_apply=%region_0.0 | all-reduce | flops 16 | bytes 128 | tf_op jit(solution)/shard_map/psum | solution.py:58
  119.1 5.4 %convolution_subtract_fusion = f32[4,81920]{1,0:T(4,128)S(1)} fusion(f32[1,4,640,128]{3,2,1,0:T(8,128)S(1)} %bitcast.88, f32[1,81920]{1,0:T(1,128)} %bitcast.93, f32[1,81920]{1,0:T(1,128)} %bitcast.92, f32[1,81920]{1,0:T(1,128)S(1)} %bitcast.91, f32[1,81920]{1,0:T(1,128)S(1)} %bitcast.90, f32[4,4]{0,1:T(4,128)S(1)} %psum.14), kind=kOutput, calls=%fused_computation | convolution fusion | flops 17039376 | bytes 3932224 | tf_op jit(solution)/shard_map/dot_general | solution.py:59
  124.5 5.7 %fusion.41 = f32[4,4]{0,1:T(4,128)S(1)} fusion(f32[4,81920]{1,0:T(4,128)S(1)} %convolution_subtract_fusion), kind=kOutput, calls=%fused_computation.89 | convolution fusion | flops 15728640 | bytes 1310784 | tf_op jit(solution)/shard_map/dot_general | solution.py:60
  130.2 42.4 %psum.15 = f32[4,4]{0,1:T(4,128)S(1)} all-reduce(f32[4,4]{0,1:T(4,128)S(1)} %fusion.41), channel_id=1, replica_groups=mesh['stream'=16,'span'=2] {'stream','span'}, use_global_device_ids=true, to_apply=%region_1.0 | all-reduce | flops 16 | bytes 128 | tf_op jit(solution)/shard_map/psum | solution.py:61
  172.7 0.4 cholesky.18
  173.1 0.6 compare_reduce_fusion
  173.7 0.6 select_bitcast_fusion
  174.7 2.8 %fusion.24 = f32[4,10,8,8,128]{4,0,3,2,1:T(4,128)S(1)} fusion(f32[10,8,8,128,4]{3,4,2,1,0:T(4,128)S(1)} %bitcast.83, f32[1,4,4]{1,2,0:T(4,128)S(1)} %custom-call.7), kind=kOutput, calls=%fused_computation.63 | convolution fusion | flops 15728640 | bytes 2621504 | tf_op jit(solution)/shard_map/jit(_solve_triangular)/triangular_solve | solution.py:63
  177.5 1.2 copy.59
  178.7 0.7 copy.58
  179.4 0.7 copy.57
  (44 shorter events, 2.6 us)
Async XLA Ops:
  0.6 24.5 %copy-start = (f32[10,10]{1,0:T(8,128)S(1)}, f32[10,10]{1,0:T(8,128)}, u32[]{:S(2)}) copy-start(f32[10,10]{1,0:T(8,128)} %param.8) | copy-start | bytes 1204
  5.1 7.4 %collective-permute-start = (f32[10,1,8,128]{3,0,2,1:T(8,128)S(1)}, f32[10,1,8,128]{3,0,2,1:T(8,128)S(1)}, u32[]{:S(2)}, u32[]{:S(2)}) collective-permute-start(f32[10,1,8,128]{3,0,2,1:T(8,128)S(1)} %get-tuple-element.33), channel_id=1, source_target_pairs={{2,0},{4,2},{6,4},{8,6},{10,8},{12,10},{14,12},{16,14},{18,16},{20... | collective-permute-start | bytes 122888 | tf_op jit(solution)/shard_map/ppermute | solution.py:17
  10.6 6.4 %collective-permute-start.1 = (f32[10,1,8,128]{3,0,2,1:T(8,128)S(1)}, f32[10,1,8,128]{3,0,2,1:T(8,128)S(1)}, u32[]{:S(2)}, u32[]{:S(2)}) collective-permute-start(f32[10,1,8,128]{3,0,2,1:T(8,128)S(1)} %get-tuple-element.32), channel_id=1, source_target_pairs={{0,2},{2,4},{4,6},{6,8},{8,10},{10,12},{12,14},{14,16},{16,18},{18... | collective-permute-start | bytes 122888 | tf_op jit(solution)/shard_map/ppermute | solution.py:16
  17.9 2.8 %copy-start.4 = (f32[8,8,128]{2,1,0:T(8,128)S(1)}, f32[8,8,128]{2,1,0:T(8,128)}, u32[]{:S(2)}) copy-start(f32[8,8,128]{2,1,0:T(8,128)} %param.9) | copy-start | bytes 98308
  17.9 4.1 %collective-permute-start.2 = (f32[10,10,8,1]{1,2,3,0:T(8,128)S(1)}, f32[10,10,8,1]{1,2,3,0:T(8,128)S(1)}, u32[]{:S(2)}, u32[]{:S(2)}) collective-permute-start(f32[10,10,8,1]{1,2,3,0:T(8,128)S(1)} %copy.31), channel_id=1, source_target_pairs={{1,0},{0,1},{3,2},{2,3},{5,4},{4,5},{7,6},{6,7},{9,8},{8,9},{11,10... | collective-permute-start | bytes 9608 | tf_op jit(solution)/shard_map/ppermute | solution.py:17
  20.1 5.1 %copy-start.5 = (f32[8,8,128]{2,1,0:T(8,128)S(1)}, f32[8,8,128]{2,1,0:T(8,128)}, u32[]{:S(2)}) copy-start(f32[8,8,128]{2,1,0:T(8,128)} %param.11) | copy-start | bytes 98308
  20.1 5.1 %copy-start.6 = (f32[8,8,128]{2,1,0:T(8,128)S(1)}, f32[8,8,128]{2,1,0:T(8,128)}, u32[]{:S(2)}) copy-start(f32[8,8,128]{2,1,0:T(8,128)} %param.10) | copy-start | bytes 98308
  20.1 4.1 %collective-permute-start.3 = (f32[10,10,8,1]{1,2,3,0:T(8,128)S(1)}, f32[10,10,8,1]{1,2,3,0:T(8,128)S(1)}, u32[]{:S(2)}, u32[]{:S(2)}) collective-permute-start(f32[10,10,8,1]{1,2,3,0:T(8,128)S(1)} %copy.33), channel_id=1, source_target_pairs={{0,1},{1,0},{2,3},{3,2},{4,5},{5,4},{6,7},{7,6},{8,9},{9,8},{10,11... | collective-permute-start | bytes 9608 | tf_op jit(solution)/shard_map/ppermute | solution.py:16
  26.1 2.0 %collective-permute-start.4 = (f32[10,1,8,128]{3,0,2,1:T(8,128)S(1)}, f32[10,1,8,128]{3,0,2,1:T(8,128)S(1)}, u32[]{:S(2)}, u32[]{:S(2)}) collective-permute-start(f32[10,1,8,128]{3,0,2,1:T(8,128)S(1)} %get-tuple-element.29), channel_id=1, source_target_pairs={{2,0},{4,2},{6,4},{8,6},{10,8},{12,10},{14,12},{16,14},{18,16},{20... | collective-permute-start | bytes 122888 | tf_op jit(solution)/shard_map/ppermute | solution.py:17
  26.1 6.4 %collective-permute-start.5 = (f32[10,1,8,128]{3,0,2,1:T(8,128)S(1)}, f32[10,1,8,128]{3,0,2,1:T(8,128)S(1)}, u32[]{:S(2)}, u32[]{:S(2)}) collective-permute-start(f32[10,1,8,128]{3,0,2,1:T(8,128)S(1)} %get-tuple-element.28), channel_id=1, source_target_pairs={{0,2},{2,4},{4,6},{6,8},{8,10},{10,12},{12,14},{14,16},{16,18},{18... | collective-permute-start | bytes 122888 | tf_op jit(solution)/shard_map/ppermute | solution.py:16
  33.5 4.0 %collective-permute-start.6 = (f32[10,10,8,1]{1,2,3,0:T(8,128)S(1)}, f32[10,10,8,1]{1,2,3,0:T(8,128)S(1)}, u32[]{:S(2)}, u32[]{:S(2)}) collective-permute-start(f32[10,10,8,1]{1,2,3,0:T(8,128)S(1)} %copy.35), channel_id=1, source_target_pairs={{1,0},{0,1},{3,2},{2,3},{5,4},{4,5},{7,6},{6,7},{9,8},{8,9},{11,10... | collective-permute-start | bytes 9608 | tf_op jit(solution)/shard_map/ppermute | solution.py:17
  34.7 4.0 %collective-permute-start.7 = (f32[10,10,8,1]{1,2,3,0:T(8,128)S(1)}, f32[10,10,8,1]{1,2,3,0:T(8,128)S(1)}, u32[]{:S(2)}, u32[]{:S(2)}) collective-permute-start(f32[10,10,8,1]{1,2,3,0:T(8,128)S(1)} %copy.37), channel_id=1, source_target_pairs={{0,1},{1,0},{2,3},{3,2},{4,5},{5,4},{6,7},{7,6},{8,9},{9,8},{10,11... | collective-permute-start | bytes 9608 | tf_op jit(solution)/shard_map/ppermute | solution.py:16
  40.7 2.0 %collective-permute-start.8 = (f32[10,1,8,128]{3,0,2,1:T(8,128)S(1)}, f32[10,1,8,128]{3,0,2,1:T(8,128)S(1)}, u32[]{:S(2)}, u32[]{:S(2)}) collective-permute-start(f32[10,1,8,128]{3,0,2,1:T(8,128)S(1)} %get-tuple-element.25), channel_id=1, source_target_pairs={{2,0},{4,2},{6,4},{8,6},{10,8},{12,10},{14,12},{16,14},{18,16},{20... | collective-permute-start | bytes 122888 | tf_op jit(solution)/shard_map/ppermute | solution.py:17
  40.7 6.6 %collective-permute-start.9 = (f32[10,1,8,128]{3,0,2,1:T(8,128)S(1)}, f32[10,1,8,128]{3,0,2,1:T(8,128)S(1)}, u32[]{:S(2)}, u32[]{:S(2)}) collective-permute-start(f32[10,1,8,128]{3,0,2,1:T(8,128)S(1)} %get-tuple-element.24), channel_id=1, source_target_pairs={{0,2},{2,4},{4,6},{6,8},{8,10},{10,12},{12,14},{14,16},{16,18},{18... | collective-permute-start | bytes 122888 | tf_op jit(solution)/shard_map/ppermute | solution.py:16
  48.2 4.0 %collective-permute-start.10 = (f32[10,10,8,1]{1,2,3,0:T(8,128)S(1)}, f32[10,10,8,1]{1,2,3,0:T(8,128)S(1)}, u32[]{:S(2)}, u32[]{:S(2)}) collective-permute-start(f32[10,10,8,1]{1,2,3,0:T(8,128)S(1)} %copy.39), channel_id=1, source_target_pairs={{1,0},{0,1},{3,2},{2,3},{5,4},{4,5},{7,6},{6,7},{9,8},{8,9},{11,10... | collective-permute-start | bytes 9608 | tf_op jit(solution)/shard_map/ppermute | solution.py:17
  50.4 4.0 %collective-permute-start.11 = (f32[10,10,8,1]{1,2,3,0:T(8,128)S(1)}, f32[10,10,8,1]{1,2,3,0:T(8,128)S(1)}, u32[]{:S(2)}, u32[]{:S(2)}) collective-permute-start(f32[10,10,8,1]{1,2,3,0:T(8,128)S(1)} %copy.41), channel_id=1, source_target_pairs={{0,1},{1,0},{2,3},{3,2},{4,5},{5,4},{6,7},{7,6},{8,9},{9,8},{10,11... | collective-permute-start | bytes 9608 | tf_op jit(solution)/shard_map/ppermute | solution.py:16
  57.4 2.2 %collective-permute-start.12 = (f32[10,1,8,128]{3,0,2,1:T(8,128)S(1)}, f32[10,1,8,128]{3,0,2,1:T(8,128)S(1)}, u32[]{:S(2)}, u32[]{:S(2)}) collective-permute-start(f32[10,1,8,128]{3,0,2,1:T(8,128)S(1)} %get-tuple-element.21), channel_id=1, source_target_pairs={{2,0},{4,2},{6,4},{8,6},{10,8},{12,10},{14,12},{16,14},{18,16},{20... | collective-permute-start | bytes 122888 | tf_op jit(solution)/shard_map/ppermute | solution.py:17
  57.4 6.4 %collective-permute-start.13 = (f32[10,1,8,128]{3,0,2,1:T(8,128)S(1)}, f32[10,1,8,128]{3,0,2,1:T(8,128)S(1)}, u32[]{:S(2)}, u32[]{:S(2)}) collective-permute-start(f32[10,1,8,128]{3,0,2,1:T(8,128)S(1)} %get-tuple-element.20), channel_id=1, source_target_pairs={{0,2},{2,4},{4,6},{6,8},{8,10},{10,12},{12,14},{14,16},{16,18},{18... | collective-permute-start | bytes 122888 | tf_op jit(solution)/shard_map/ppermute | solution.py:16
  64.8 4.4 %collective-permute-start.14 = (f32[10,10,8,1]{1,2,3,0:T(8,128)S(1)}, f32[10,10,8,1]{1,2,3,0:T(8,128)S(1)}, u32[]{:S(2)}, u32[]{:S(2)}) collective-permute-start(f32[10,10,8,1]{1,2,3,0:T(8,128)S(1)} %copy.43), channel_id=1, source_target_pairs={{1,0},{0,1},{3,2},{2,3},{5,4},{4,5},{7,6},{6,7},{9,8},{8,9},{11,10... | collective-permute-start | bytes 9608 | tf_op jit(solution)/shard_map/ppermute | solution.py:17
  66.0 4.2 %collective-permute-start.15 = (f32[10,10,8,1]{1,2,3,0:T(8,128)S(1)}, f32[10,10,8,1]{1,2,3,0:T(8,128)S(1)}, u32[]{:S(2)}, u32[]{:S(2)}) collective-permute-start(f32[10,10,8,1]{1,2,3,0:T(8,128)S(1)} %copy.45), channel_id=1, source_target_pairs={{0,1},{1,0},{2,3},{3,2},{4,5},{5,4},{6,7},{7,6},{8,9},{9,8},{10,11... | collective-permute-start | bytes 9608 | tf_op jit(solution)/shard_map/ppermute | solution.py:16
  73.1 1.3 copy-start.1
  74.4 44.7 %copy-start.2 = (f32[10,8,8,128]{3,2,1,0:T(8,128)S(1)}, f32[10,8,8,128]{3,2,1,0:T(8,128)}, u32[]{:S(2)}) copy-start(f32[10,8,8,128]{3,2,1,0:T(8,128)} %copy.49) | copy-start | bytes 983044
  74.4 44.7 %copy-start.3 = (f32[10,8,8,128]{3,2,1,0:T(8,128)S(1)}, f32[10,8,8,128]{3,2,1,0:T(8,128)}, u32[]{:S(2)}) copy-start(f32[10,8,8,128]{3,2,1,0:T(8,128)} %copy.50) | copy-start | bytes 983044
where the time goes:
time: 180 us
  blocking collectives  79.4 us (44%)
  matrix products  30.6 us (17%)
  waiting for transfers between devices  28.3 us (16%)
  local copies, waits for them, and re-layouts  22.8 us (13%)
  starting transfers between devices  15.7 us (9%)
  other arithmetic  2.38 us (1%)
    psum x1, blocking collectives, on_device(): gram = lax.psum(local_gram, ('stream', 'span')) / total  42.4 us
    psum x1, blocking collectives, on_device(): proj = lax.psum(local_proj, ('stream', 'span')) / total  37.1 us
    ppermute x8, waiting for transfers between devices, padded(): before = lax.ppermute(last, axis, up)  20.6 us
    ppermute x8, starting transfers between devices, padded(): after = lax.ppermute(leading, axis, down)  9.91 us
    ppermute x8, waiting for transfers between devices, padded(): after = lax.ppermute(leading, axis, down)  7.67 us
    dot_general x1, matrix products, on_device(): jnp.dot(flat_basis, flat_new.T, precision=lax.Precision.HIGHEST)  6.78 us
    ppermute x8, starting transfers between devices, padded(): before = lax.ppermute(last, axis, up)  5.75 us
    dot_general x4, matrix products, advance(): jnp.einsum('fg,gxyz->fxyz', mixing_matrix, center_part, precision=lax.Pre...  5.73 us
  transfers between devices with their start and end apart: 16, of which 13 were waited for; matrix products, arithmetic and copies ran while one was open for 6% of the time, Pallas kernels for 0%

commit v1 on v0

v1 whole, which is shorter than its diff:
```python
import functools

import jax
import jax.numpy as jnp
from jax import lax
from jax.experimental import pallas as pl
from jax.experimental.pallas import tpu as pltpu
from jax.sharding import PartitionSpec as P

STEPS = 4
DEEP = 4
WIDE = 2 * DEEP
MESH = pl.DeviceIdType.MESH


def total(terms):
    terms = list(terms)
    while len(terms) > 1:
        pairs = [terms[i] + terms[i + 1] for i in range(0, len(terms) - 1, 2)]
        terms = pairs + terms[len(terms) - len(terms) % 2 :]
    return terms[0]


def span_offsets(span):
    return () if span == 1 else ((1,) if span == 2 else (-1, 1))


def partners(span):
    dzs = span_offsets(span)
    return [(dx, 0) for dx in (-1, 1)] + [(0, dz) for dz in dzs] + [
        (dx, dz) for dx in (-1, 1) for dz in dzs
    ]


def krylov_kernel(
    streams, spans,
    coeffs, mix, basis, base, span_speed, gain,
    krylov_out, sums_out,
    ext, state, held, pack, packs, strips, coef, strip_coef, acc, rows, gathered,
    in_sem, out_sem, send_sem, recv_sem, row_send, row_recv,
):
    m, fields, planes = basis.shape[0], basis.shape[1], basis.shape[2]
    steps = STEPS
    lanes = basis.shape[4]
    n = streams * spans
    all_fields = fields + 3
    sx, sz = lax.axis_index("stream"), lax.axis_index("span")
    me = sx * spans + sz

    def device(dx, dz):
        return (lax.rem(sx + dx + streams, streams), lax.rem(sz + dz + spans, spans))

    barrier = pltpu.get_barrier_semaphore()

    def greet(d, carry):
        other = lax.rem(me + d, n)
        pl.semaphore_signal(
            barrier, inc=1, device_id=(other // spans, lax.rem(other, spans)), device_id_type=MESH
        )
        return carry

    own = pl.ds(DEEP, planes)
    loads = [
        pltpu.make_async_copy(basis.at[j], held.at[j], in_sem.at[j]) for j in range(m)
    ] + [
        pltpu.make_async_copy(ref, ext.at[fields + i, own], in_sem.at[m + i])
        for i, ref in enumerate((base, span_speed, gain))
    ]
    for load in loads:
        load.start()
    lax.fori_loop(1, n, greet, 0)

    lane = lax.broadcasted_iota(jnp.int32, (8, lanes), 1)
    row = lax.broadcasted_iota(jnp.int32, (8, lanes), 0)

    def packed(field):
        out = jnp.zeros((8, lanes), jnp.float32)
        for x in range(planes):
            at = WIDE * (x + DEEP)
            moved = pltpu.roll(ext[field, DEEP + x], DEEP + at, 1)
            out = jnp.where((lane >= at) & (lane < at + WIDE), moved, out)
        pack[field] = out

    for load in loads:
        load.wait()

    def start_field(f, carry):
        for x in range(planes):
            ext[f, DEEP + x] = total(coeffs[j] * held[j, f, x] for j in range(m))
        packed(f)
        return carry

    lax.fori_loop(0, fields, start_field, 0)
    for i in range(3):
        packed(fields + i)

    pl.semaphore_wait(barrier, n - 1)

    sends = []

    def send(src, dst, dx, dz):
        i = len(sends)
        copy = pltpu.make_async_remote_copy(
            src_ref=src, dst_ref=dst, send_sem=send_sem.at[i], recv_sem=recv_sem.at[i],
            device_id=device(dx, dz), device_id_type=MESH,
        )
        copy.start()
        sends.append(copy)

    send(ext.at[:, pl.ds(planes, DEEP)], ext.at[:, pl.ds(0, DEEP)], 1, 0)
    send(ext.at[:, pl.ds(DEEP, DEEP)], ext.at[:, pl.ds(planes + DEEP, DEEP)], -1, 0)
    slots = partners(spans)
    for i, (dx, dz) in enumerate(slots):
        send(pack, packs.at[i], -dx, -dz)

    upper = [(i, j) for i in range(m) for j in range(i, m)]
    krylov_pairs = [(k, l) for k in range(steps) for l in range(k, steps)]
    zero = jnp.zeros((8, lanes), jnp.float32)

    def basis_products(f, sums):
        for x in range(planes):
            b = [held[j, f, x] for j in range(m)]
            sums = [s + b[i] * b[j] for s, (i, j) in zip(sums, upper)]
        return sums

    basis_sums = lax.fori_loop(0, fields, basis_products, [zero] * len(upper))
    first = m * steps + len(krylov_pairs)
    for i, s in enumerate(basis_sums):
        acc[first + i] = s

    for copy in sends:
        copy.wait_recv()

    def cooked(u, w):
        return (
            0.05 - 0.5 * u, 0.05 + 0.5 * u, 0.05 - 0.5 * w, 0.05 + 0.5 * w
        )

    for x in range(1, planes + 2 * DEEP - 1):
        for i, value in enumerate(cooked(ext[fields, x], ext[fields + 1, x])):
            coef[i, x] = value

    half = DEEP * WIDE
    inside = (lane >= half) & (lane < half + planes * WIDE)
    left_part = lane % WIDE < DEEP

    def strip_pair(f):
        def whole(dz):
            here = pack[f] if dz == 0 else packs[slots.index((0, dz)), f]
            before = packs[slots.index((-1, dz)), f]
            after = packs[slots.index((1, dz)), f]
            beside = jnp.where(lane < lanes // 2, after, before)
            return jnp.where(inside, here, pltpu.roll(beside, lanes // 2, 1))

        mine = whole(0)
        dzs = span_offsets(spans)
        left = whole(dzs[0]) if dzs else mine
        right = left if len(dzs) < 2 else whole(dzs[1])
        return jnp.where(left_part, left, mine), jnp.where(left_part, mine, right)

    def build_strips(f, carry):
        for s, value in enumerate(strip_pair(f)):
            strips[0, f, s] = value
        return carry

    lax.fori_loop(0, fields, build_strips, 0)
    us, ws, gs = (strip_pair(fields + i) for i in range(3))
    for s in range(2):
        for i, value in enumerate(cooked(us[s], ws[s]) + (gs[s],)):
            strip_coef[i, s] = value

    def walls(v):
        up = jnp.where(row < 7, pltpu.roll(v, 7, 0), 0.0)
        down = jnp.where(row > 0, pltpu.roll(v, 1, 0), 0.0)
        return up + down

    def read(k, f, x):
        return ext[f, x] if k == 0 else state[k - 1, f, x]

    writes = []
    for k in range(steps):
        lo, hi = 1 + k, planes + 2 * DEEP - 1 - k

        def field_pair(h, carry, k=k, lo=lo, hi=hi):
            pair = [2 * h, 2 * h + 1]
            weights = [[mix[f, g] for g in range(fields)] for f in pair]
            edges = [
                jnp.where(lane % WIDE == DEEP - 1, strips[k, f, 0],
                          pltpu.roll(strips[k, f, 1], lanes - 2, 1))
                for f in pair
            ]
            for x in range(lo, hi):
                vs = [read(k, g, x) for g in range(fields)]
                for f, weight, edge in zip(pair, weights, edges):
                    mixed = total(a * v for a, v in zip(weight, vs))
                    v = read(k, f, x)
                    rim = pltpu.roll(edge, (2 * lanes - (WIDE * x + DEEP - 1)) % lanes, 1)
                    ahead = jnp.where(lane == lanes - 1, rim, pltpu.roll(v, lanes - 1, 1))
                    behind = jnp.where(lane == 0, rim, pltpu.roll(v, 1, 1))
                    state[k, f, x] = (
                        (coef[0, x] * read(k, f, x + 1) + coef[1, x] * read(k, f, x - 1))
                        + (coef[2, x] * ahead + coef[3, x] * behind)
                        + (0.05 * walls(v) - 0.3 * v)
                        + ext[fields + 2, x] * mixed
                    )
            if k < steps - 1:
                for s in range(2):
                    vs = [strips[k, g, s] for g in range(fields)]
                    for f, weight in zip(pair, weights):
                        mixed = total(a * v for a, v in zip(weight, vs))
                        v = strips[k, f, s]
                        strips[k + 1, f, s] = (
                            strip_coef[0, s] * pltpu.roll(v, lanes - WIDE, 1)
                            + strip_coef[1, s] * pltpu.roll(v, WIDE, 1)
                            + strip_coef[2, s] * pltpu.roll(v, lanes - 1, 1)
                            + strip_coef[3, s] * pltpu.roll(v, 1, 1)
                            + (0.05 * walls(v) - 0.3 * v)
                            + strip_coef[4, s] * mixed
                        )
            return carry

        lax.fori_loop(0, fields // 2, field_pair, 0)
        write = pltpu.make_async_copy(state.at[k, :, own], krylov_out.at[k], out_sem.at[k])
        write.start()
        writes.append(write)

    def new_products(f, sums):
        for x in range(planes):
            b = [held[j, f, x] for j in range(m)]
            v = [state[k, f, DEEP + x] for k in range(steps)]
            terms = [b[j] * v[k] for j in range(m) for k in range(steps)]
            terms += [v[k] * v[l] for k, l in krylov_pairs]
            sums = [s + t for s, t in zip(sums, terms)]
        return sums

    new_sums = lax.fori_loop(0, fields, new_products, [zero] * first)
    count = first + len(upper)
    for i, s in enumerate(new_sums):
        rows[pl.ds(i, 1)] = jnp.sum(s, axis=0, keepdims=True)
    for i in range(first, count):
        rows[pl.ds(i, 1)] = jnp.sum(acc[i], axis=0, keepdims=True)
    for i in range(count, rows.shape[0]):
        rows[pl.ds(i, 1)] = jnp.zeros((1, lanes), jnp.float32)
    sums = jnp.sum(rows[...], axis=1, keepdims=True)
    at = lax.broadcasted_iota(jnp.int32, rows.shape, 0)
    spot = lax.broadcasted_iota(jnp.int32, rows.shape, 1)
    gathered[me] = jnp.sum(jnp.where(at == spot, sums, 0.0), axis=0, keepdims=True)

    def row_copy(d):
        other = lax.rem(me + d, n)
        return pltpu.make_async_remote_copy(
            src_ref=gathered.at[me], dst_ref=gathered.at[me], send_sem=row_send, recv_sem=row_recv,
            device_id=(other // spans, lax.rem(other, spans)), device_id_type=MESH,
        )

    def share(d, carry):
        row_copy(d).start()
        return carry

    lax.fori_loop(1, n, share, 0)
    others = gathered.at[pl.ds(0, n - 1)]
    everyone = pltpu.make_async_remote_copy(
        src_ref=others, dst_ref=others, send_sem=row_send, recv_sem=row_recv,
        device_id=device(1, 0), device_id_type=MESH,
    )
    everyone.wait_recv()
    sums_out[...] = jnp.sum(gathered[...], axis=0)
    everyone.wait_send()
    for copy in sends:
        copy.wait_send()
    for write in writes:
        write.wait()


def finish_kernel(
    ntot, chunks,
    sums, basis, krylov,
    proj_out, rfactor_out, new_out,
    held, vectors, result, basis_sem, krylov_sem, out_sem,
):
    m, fields, planes = basis.shape[0], basis.shape[1], basis.shape[2]
    steps = krylov.shape[0]
    part = fields // chunks

    def piece(c):
        return pl.ds(c * part, part)

    loads = []
    for c in range(chunks):
        loads.append((
            pltpu.make_async_copy(basis.at[:, piece(c)], held.at[:, piece(c)], basis_sem.at[c]),
            pltpu.make_async_copy(krylov.at[:, piece(c)], vectors.at[:, piece(c)], krylov_sem.at[c]),
        ))
        for load in loads[-1]:
            load.start()

    shape = (8, basis.shape[4])
    row = sums[...] * (1.0 / ntot)

    def value(i):
        return jnp.broadcast_to(row[:, i : i + 1], shape)

    p = [[value(steps * j + k) for k in range(steps)] for j in range(m)]
    at = m * steps
    kk, bb = {}, {}
    for k in range(steps):
        for l in range(k, steps):
            kk[k, l] = value(at)
            at += 1
    for i in range(m):
        for j in range(i, m):
            bb[i, j] = bb[j, i] = value(at)
            at += 1
    q = [
        [2.0 * p[i][l] - total(bb[i, j] * p[j][l] for j in range(m)) for l in range(steps)]
        for i in range(m)
    ]
    low, inverse = {}, []
    for l in range(steps):
        for k in range(l, steps):
            g = kk[l, k] - total(p[i][l] * q[i][k] for i in range(m))
            for j in range(l):
                g = g - low[k, j] * low[l, j]
            if k == l:
                low[l, l] = jnp.sqrt(g)
                inverse.append(1.0 / low[l, l])
            else:
                low[k, l] = g * inverse[l]

    x = lax.broadcasted_iota(jnp.int32, shape, 0)
    y = lax.broadcasted_iota(jnp.int32, shape, 1)
    proj = jnp.zeros(shape, jnp.float32)
    for j in range(m):
        for k in range(steps):
            proj = jnp.where((x == j) & (y == k), p[j][k], proj)
    proj_out[...] = proj[:m, :steps]
    factor = jnp.zeros(shape, jnp.float32)
    for k, l in low:
        factor = jnp.where((x == l) & (y == k), low[k, l], factor)
    rfactor_out[...] = factor[:steps, :steps]

    writes = []
    for c in range(chunks):
        for load in loads[c]:
            load.wait()

        def one(i, carry, c=c):
            f = c * part + i
            for s in range(planes):
                b = [held[j, f, s] for j in range(m)]
                done = []
                for k in range(steps):
                    v = vectors[k, f, s] - total(p[j][k] * b[j] for j in range(m))
                    for l in range(k):
                        v = v - low[k, l] * done[l]
                    done.append(v * inverse[k])
                    result[k, f, s] = done[k]
            return carry

        lax.fori_loop(0, part, one, 0)
        write = pltpu.make_async_copy(
            result.at[:, piece(c)], new_out.at[:, piece(c)], out_sem.at[c]
        )
        write.start()
        writes.append(write)
    for write in writes:
        write.wait()


def on_device(streams, spans, basis, coeffs, mixing_matrix, base_speed, span_speed, polymer_gain):
    m, fields, planes, height, lanes = basis.shape
    n = streams * spans
    f32 = jnp.float32
    deep = planes + 2 * DEEP
    count = m * STEPS + STEPS * (STEPS + 1) // 2 + m * (m + 1) // 2
    padded = -(-count // 8) * 8
    links = 2 + len(partners(spans))
    smem = pl.BlockSpec(memory_space=pltpu.SMEM)
    hbm = pl.BlockSpec(memory_space=pl.ANY)
    vmem = pl.BlockSpec(memory_space=pltpu.VMEM)
    vector = (fields, planes, height, lanes)
    krylov, sums = pl.pallas_call(
        functools.partial(krylov_kernel, streams, spans),
        out_shape=(
            jax.ShapeDtypeStruct((STEPS,) + vector, f32),
            jax.ShapeDtypeStruct((1, lanes), f32),
        ),
        in_specs=[smem, smem, hbm, hbm, hbm, hbm],
        out_specs=(hbm, vmem),
        scratch_shapes=[
            pltpu.VMEM((fields + 3, deep, height, lanes), f32),
            pltpu.VMEM((STEPS, fields, deep, height, lanes), f32),
            pltpu.VMEM((m,) + vector, f32),
            pltpu.VMEM((fields + 3, height, lanes), f32),
            pltpu.VMEM((links - 2, fields + 3, height, lanes), f32),
            pltpu.VMEM((STEPS, fields, 2, height, lanes), f32),
            pltpu.VMEM((4, deep, height, lanes), f32),
            pltpu.VMEM((5, 2, height, lanes), f32),
            pltpu.VMEM((count, height, lanes), f32),
            pltpu.VMEM((padded, lanes), f32),
            pltpu.VMEM((n, 1, lanes), f32),
            pltpu.SemaphoreType.DMA((m + 3,)),
            pltpu.SemaphoreType.DMA((STEPS,)),
            pltpu.SemaphoreType.DMA((links,)),
            pltpu.SemaphoreType.DMA((links,)),
            pltpu.SemaphoreType.DMA,
            pltpu.SemaphoreType.DMA,
        ],
        compiler_params=pltpu.CompilerParams(
            collective_id=0, has_side_effects=True, vmem_limit_bytes=24 * 2**20
        ),
        name="krylov",
    )(coeffs, mixing_matrix, basis, base_speed, span_speed, polymer_gain)
    chunks = 5 if fields % 5 == 0 else 1
    return pl.pallas_call(
        functools.partial(finish_kernel, float(m and basis[0].size * n), chunks),
        out_shape=(
            jax.ShapeDtypeStruct((m, STEPS), f32),
            jax.ShapeDtypeStruct((STEPS, STEPS), f32),
            jax.ShapeDtypeStruct((STEPS,) + vector, f32),
        ),
        in_specs=[vmem, hbm, hbm],
        out_specs=(vmem, vmem, hbm),
        scratch_shapes=[
            pltpu.VMEM((m,) + vector, f32),
            pltpu.VMEM((STEPS,) + vector, f32),
            pltpu.VMEM((STEPS,) + vector, f32),
            pltpu.SemaphoreType.DMA((chunks,)),
            pltpu.SemaphoreType.DMA((chunks,)),
            pltpu.SemaphoreType.DMA((chunks,)),
        ],
        compiler_params=pltpu.CompilerParams(vmem_limit_bytes=24 * 2**20),
        name="finish",
    )(sums, basis, krylov)


def solution(mesh):
    placed = (
        P(None, None, "stream", None, "span"),
        P(),
        P(),
        P("stream", None, "span"),
        P("stream", None, "span"),
        P("stream", None, "span"),
    )
    return jax.shard_map(
        functools.partial(on_device, mesh.shape["stream"], mesh.shape["span"]),
        mesh=mesh,
        in_specs=placed,
        out_specs=(P(), P(), P(None, None, "stream", None, "span")),
        check_vma=False,
    )
```

time: 180 us -> 35.8 us (0.20)
  blocking collectives: 79.4 us -> 0 us
  matrix products: 30.6 us -> 0 us
  Pallas kernels: 0 us -> 29.7 us
  waiting for transfers between devices: 28.3 us -> 0 us
  local copies, waits for them, and re-layouts: 22.8 us -> 4.94 us
  starting transfers between devices: 15.7 us -> 0 us
  other arithmetic: 2.38 us -> 0 us
    psum x2 -> x0, blocking collectives: 79.4 us -> none  [the longest x1 42.4 us: on_device(): gram = lax.psum(local_gram, ('stream', 'span')) / total]
    pallas_call x0 -> x2, Pallas kernels: none -> 29.7 us  [the longest x1 27.4 us: on_device(): pl.pallas_call(functools.partial(krylov_kernel, streams, spans), out_shap...]
    ppermute x16 -> x0, waiting for transfers between devices: 28.3 us -> none  [the longest x8 20.6 us: padded(): before = lax.ppermute(last, axis, up)]
    dot_general x8 -> x0, matrix products: 27.8 us -> none  [the longest x1 6.78 us: on_device(): jnp.dot(flat_basis, flat_new.T, precision=lax.Precision.HIGHEST)]
    ppermute x16 -> x0, starting transfers between devices: 15.7 us -> none  [the longest x8 9.91 us: padded(): after = lax.ppermute(leading, axis, down)]
    ppermute x8 -> x0, local copies, waits for them, and re-layouts: 7.81 us -> none  [the longest x4 3.91 us: padded(): before = lax.ppermute(last, axis, up)]
    slice x20 -> x0, local copies, waits for them, and re-layouts: 7.64 us -> none  [the longest x12 3.41 us: padded(): last = lax.slice_in_dim(value, length - width, length, axis=dim)]
    add x4 -> x0, local copies, waits for them, and re-layouts: 3.33 us -> none  [advance(): -base_speed * (forward_x - backward_x) * 0.5]
  transfers between devices with their start and end apart: 16 -> 0, of which waited for: 13 -> 0; matrix products, arithmetic and copies ran while one was open for 6% -> 0% of each run, Pallas kernels for 0% -> 0%
where the time goes in v1:
time: 35.8 us; the launch traced here: 35.3 us
  Pallas kernels  29.7 us (83%)
  local copies, waits for them, and re-layouts  4.94 us (14%)
  between operations  0.66 us (2%)
    pallas_call x1, Pallas kernels, on_device(): pl.pallas_call(functools.partial(krylov_kernel, streams, spans), out_shap...  27.4 us
    unnamed x14, local copies, waits for them, and re-layouts  4.94 us
    pallas_call x1, Pallas kernels, on_device(): pl.pallas_call(functools.partial(finish_kernel, float(m and basis[0].size...  2.37 us

profile of v1, /device:TPU:0, one launch (start us, length us, event | category | flops | bytes accessed | tf_op | source)
XLA Modules:
  0.0 35.3 jit_solution(16629483372631362304)
XLA Ops:
  0.6 0.0 copy-start
  0.6 1.3 %copy-done = f32[4,10,8,8,128]{4,3,2,1,0:T(8,128)S(1)} copy-done((f32[4,10,8,8,128]{4,3,2,1,0:T(8,128)S(1)}, f32[4,10,8,8,128]{4,3,2,1,0:T(8,128)}, u32[]{:S(2)}) %copy-start) | copy-done | bytes 1310744
  1.9 0.0 copy-start.2
  2.0 0.8 %copy-done.2 = f32[8,8,128]{2,1,0:T(8,128)S(1)} copy-done((f32[8,8,128]{2,1,0:T(8,128)S(1)}, f32[8,8,128]{2,1,0:T(8,128)}, u32[]{:S(2)}) %copy-start.2) | copy-done | bytes 32792
  2.7 0.0 copy-start.3
  2.7 0.8 %copy-done.3 = f32[8,8,128]{2,1,0:T(8,128)S(1)} copy-done((f32[8,8,128]{2,1,0:T(8,128)S(1)}, f32[8,8,128]{2,1,0:T(8,128)}, u32[]{:S(2)}) %copy-start.3) | copy-done | bytes 32792
  3.5 0.0 copy-start.4
  3.5 0.8 %copy-done.4 = f32[8,8,128]{2,1,0:T(8,128)S(1)} copy-done((f32[8,8,128]{2,1,0:T(8,128)S(1)}, f32[8,8,128]{2,1,0:T(8,128)}, u32[]{:S(2)}) %copy-start.4) | copy-done | bytes 32792
  4.2 0.0 copy-start.5
  4.2 0.7 %copy-done.5 = f32[10,10]{1,0:T(8,128)S(1)} copy-done((f32[10,10]{1,0:T(8,128)S(1)}, f32[10,10]{1,0:T(8,128)}, u32[]{:S(2)}) %copy-start.5) | copy-done | bytes 424
  4.9 0.0 copy-start.6
  4.9 0.7 %copy-done.6 = f32[4]{0:T(128)S(1)} copy-done((f32[4]{0:T(128)S(1)}, f32[4]{0:T(128)}, u32[]{:S(2)}) %copy-start.6) | copy-done | bytes 40
  5.6 0.0 copy-start.1
  5.6 27.4 %krylov.1 = (f32[4,10,8,8,128]{4,3,2,1,0:T(8,128)S(1)}, f32[1,128]{1,0:T(1,128)S(1)}) custom-call(f32[4]{0:T(128)S(1)} %copy-done.6, f32[10,10]{1,0:T(8,128)S(1)} %copy-done.5, f32[4,10,8,8,128]{4,3,2,1,0:T(8,128)S(1)} %copy-done, f32[8,8,128]{2,1,0:T(8,128)S(1)} %copy-done.2, f32[8,8,128]{2,1,0:T(8,128)S(1)} %copy-done.3, f32[8,8,128]{2,1,0:T(8,128)S(1)} %copy-done.4), custom_call_target="tpu_custom_call" | custom-call | tf_op jit(solution)/shard_map/krylov/pallas_call | solution.py:382
  33.0 0.0 copy-done.1
  33.0 2.4 %finish.1 = (f32[4,4]{1,0:T(4,128)}, f32[4,4]{1,0:T(4,128)}, f32[4,10,8,8,128]{4,3,2,1,0:T(8,128)}) custom-call(f32[1,128]{1,0:T(1,128)S(1)} %get-tuple-element.5.sums, f32[4,10,8,8,128]{4,3,2,1,0:T(8,128)S(1)} %copy-done.1, f32[4,10,8,8,128]{4,3,2,1,0:T(8,128)S(1)} %get-tuple-element.6.krylov), custom_call_target="tpu_custom_call" | custom-call | tf_op jit(solution)/shard_map/finish/pallas_call | solution.py:415
Async XLA Ops:
  0.6 1.3 %copy-start = (f32[4,10,8,8,128]{4,3,2,1,0:T(8,128)S(1)}, f32[4,10,8,8,128]{4,3,2,1,0:T(8,128)}, u32[]{:S(2)}) copy-start(f32[4,10,8,8,128]{4,3,2,1,0:T(8,128)} %basis.3) | copy-start | bytes 3932164
  1.9 0.8 %copy-start.2 = (f32[8,8,128]{2,1,0:T(8,128)S(1)}, f32[8,8,128]{2,1,0:T(8,128)}, u32[]{:S(2)}) copy-start(f32[8,8,128]{2,1,0:T(8,128)} %base.1) | copy-start | bytes 98308
  2.7 0.8 %copy-start.3 = (f32[8,8,128]{2,1,0:T(8,128)S(1)}, f32[8,8,128]{2,1,0:T(8,128)}, u32[]{:S(2)}) copy-start(f32[8,8,128]{2,1,0:T(8,128)} %span_speed.1) | copy-start | bytes 98308
  3.5 0.8 %copy-start.4 = (f32[8,8,128]{2,1,0:T(8,128)S(1)}, f32[8,8,128]{2,1,0:T(8,128)}, u32[]{:S(2)}) copy-start(f32[8,8,128]{2,1,0:T(8,128)} %gain.1) | copy-start | bytes 98308
  4.2 0.7 %copy-start.5 = (f32[10,10]{1,0:T(8,128)S(1)}, f32[10,10]{1,0:T(8,128)}, u32[]{:S(2)}) copy-start(f32[10,10]{1,0:T(8,128)} %mix.1) | copy-start | bytes 1204
  4.9 0.7 %copy-start.6 = (f32[4]{0:T(128)S(1)}, f32[4]{0:T(128)}, u32[]{:S(2)}) copy-start(f32[4]{0:T(128)} %coeffs.1) | copy-start | bytes 52
  5.6 27.4 %copy-start.1 = (f32[4,10,8,8,128]{4,3,2,1,0:T(8,128)S(1)}, f32[4,10,8,8,128]{4,3,2,1,0:T(8,128)}, u32[]{:S(2)}) copy-start(f32[4,10,8,8,128]{4,3,2,1,0:T(8,128)} %basis.3) | copy-start | bytes 3932164

commit v2 on v1

--- a/solution.py
+++ b/solution.py
@@ -34,9 +34,9 @@
 
 def krylov_kernel(
     streams, spans,
-    coeffs, mix, basis, base, span_speed, gain,
+    coeffs_in, mix_in, basis, base, span_speed, gain,
     krylov_out, sums_out,
-    ext, state, held, pack, packs, strips, coef, strip_coef, acc, rows, gathered,
+    ext, states, held, pack, packs, strips, coef, strip_coef, acc, rows, gathered, coeffs, mix,
     in_sem, out_sem, send_sem, recv_sem, row_send, row_recv,
 ):
     m, fields, planes = basis.shape[0], basis.shape[1], basis.shape[2]
@@ -65,6 +65,9 @@
     ] + [
         pltpu.make_async_copy(ref, ext.at[fields + i, own], in_sem.at[m + i])
         for i, ref in enumerate((base, span_speed, gain))
+    ] + [
+        pltpu.make_async_copy(coeffs_in, coeffs, in_sem.at[m + 3]),
+        pltpu.make_async_copy(mix_in, mix, in_sem.at[m + 4]),
     ]
     for load in loads:
         load.start()
@@ -73,26 +76,29 @@
     lane = lax.broadcasted_iota(jnp.int32, (8, lanes), 1)
     row = lax.broadcasted_iota(jnp.int32, (8, lanes), 0)
 
-    def packed(field):
+    def packed(field, values):
         out = jnp.zeros((8, lanes), jnp.float32)
         for x in range(planes):
             at = WIDE * (x + DEEP)
-            moved = pltpu.roll(ext[field, DEEP + x], DEEP + at, 1)
+            moved = pltpu.roll(values[x], DEEP + at, 1)
             out = jnp.where((lane >= at) & (lane < at + WIDE), moved, out)
         pack[field] = out
 
     for load in loads:
         load.wait()
 
+    weights = [coeffs[j] for j in range(m)]
+
     def start_field(f, carry):
+        values = [total(weights[j] * held[j, f, x] for j in range(m)) for x in range(planes)]
         for x in range(planes):
-            ext[f, DEEP + x] = total(coeffs[j] * held[j, f, x] for j in range(m))
-        packed(f)
+            ext[f, DEEP + x] = values[x]
+        packed(f, values)
         return carry
 
     lax.fori_loop(0, fields, start_field, 0)
     for i in range(3):
-        packed(fields + i)
+        packed(fields + i, [ext[fields + i, DEEP + x] for x in range(planes)])
 
     pl.semaphore_wait(barrier, n - 1)
 
@@ -160,7 +166,7 @@
 
     def build_strips(f, carry):
         for s, value in enumerate(strip_pair(f)):
-            strips[0, f, s] = value
+            strips[0][f, s] = value
         return carry
 
     lax.fori_loop(0, fields, build_strips, 0)
@@ -175,7 +181,7 @@
         return up + down
 
     def read(k, f, x):
-        return ext[f, x] if k == 0 else state[k - 1, f, x]
+        return ext[f, x] if k == 0 else states[k - 1][f, x]
 
     writes = []
     for k in range(steps):
@@ -185,8 +191,8 @@
             pair = [2 * h, 2 * h + 1]
             weights = [[mix[f, g] for g in range(fields)] for f in pair]
             edges = [
-                jnp.where(lane % WIDE == DEEP - 1, strips[k, f, 0],
-                          pltpu.roll(strips[k, f, 1], lanes - 2, 1))
+                jnp.where(lane % WIDE == DEEP - 1, strips[k][f, 0],
+                          pltpu.roll(strips[k][f, 1], lanes - 2, 1))
                 for f in pair
             ]
             for x in range(lo, hi):
@@ -197,7 +203,7 @@
                     rim = pltpu.roll(edge, (2 * lanes - (WIDE * x + DEEP - 1)) % lanes, 1)
                     ahead = jnp.where(lane == lanes - 1, rim, pltpu.roll(v, lanes - 1, 1))
                     behind = jnp.where(lane == 0, rim, pltpu.roll(v, 1, 1))
-                    state[k, f, x] = (
+                    states[k][f, x] = (
                         (coef[0, x] * read(k, f, x + 1) + coef[1, x] * read(k, f, x - 1))
                         + (coef[2, x] * ahead + coef[3, x] * behind)
                         + (0.05 * walls(v) - 0.3 * v)
@@ -205,11 +211,11 @@
                     )
             if k < steps - 1:
                 for s in range(2):
-                    vs = [strips[k, g, s] for g in range(fields)]
+                    vs = [strips[k][g, s] for g in range(fields)]
                     for f, weight in zip(pair, weights):
                         mixed = total(a * v for a, v in zip(weight, vs))
-                        v = strips[k, f, s]
-                        strips[k + 1, f, s] = (
+                        v = strips[k][f, s]
+                        strips[k + 1][f, s] = (
                             strip_coef[0, s] * pltpu.roll(v, lanes - WIDE, 1)
                             + strip_coef[1, s] * pltpu.roll(v, WIDE, 1)
                             + strip_coef[2, s] * pltpu.roll(v, lanes - 1, 1)
@@ -220,14 +226,14 @@
             return carry
 
         lax.fori_loop(0, fields // 2, field_pair, 0)
-        write = pltpu.make_async_copy(state.at[k, :, own], krylov_out.at[k], out_sem.at[k])
+        write = pltpu.make_async_copy(states[k].at[:, own], krylov_out.at[k], out_sem.at[k])
         write.start()
         writes.append(write)
 
     def new_products(f, sums):
         for x in range(planes):
             b = [held[j, f, x] for j in range(m)]
-            v = [state[k, f, DEEP + x] for k in range(steps)]
+            v = [states[k][f, DEEP + x] for k in range(steps)]
             terms = [b[j] * v[k] for j in range(m) for k in range(steps)]
             terms += [v[k] * v[l] for k, l in krylov_pairs]
             sums = [s + t for s, t in zip(sums, terms)]
@@ -276,7 +282,7 @@
     ntot, chunks,
     sums, basis, krylov,
     proj_out, rfactor_out, new_out,
-    held, vectors, result, basis_sem, krylov_sem, out_sem,
+    result, out_sem,
 ):
     m, fields, planes = basis.shape[0], basis.shape[1], basis.shape[2]
     steps = krylov.shape[0]
@@ -284,15 +290,6 @@
 
     def piece(c):
         return pl.ds(c * part, part)
-
-    loads = []
-    for c in range(chunks):
-        loads.append((
-            pltpu.make_async_copy(basis.at[:, piece(c)], held.at[:, piece(c)], basis_sem.at[c]),
-            pltpu.make_async_copy(krylov.at[:, piece(c)], vectors.at[:, piece(c)], krylov_sem.at[c]),
-        ))
-        for load in loads[-1]:
-            load.start()
 
     shape = (8, basis.shape[4])
     row = sums[...] * (1.0 / ntot)
@@ -341,16 +338,13 @@
 
     writes = []
     for c in range(chunks):
-        for load in loads[c]:
-            load.wait()
-
         def one(i, carry, c=c):
             f = c * part + i
             for s in range(planes):
-                b = [held[j, f, s] for j in range(m)]
+                b = [basis[j, f, s] for j in range(m)]
                 done = []
                 for k in range(steps):
-                    v = vectors[k, f, s] - total(p[j][k] * b[j] for j in range(m))
+                    v = krylov[k, f, s] - total(p[j][k] * b[j] for j in range(m))
                     for l in range(k):
                         v = v - low[k, l] * done[l]
                     done.append(v * inverse[k])
@@ -375,8 +369,8 @@
     count = m * STEPS + STEPS * (STEPS + 1) // 2 + m * (m + 1) // 2
     padded = -(-count // 8) * 8
     links = 2 + len(partners(spans))
-    smem = pl.BlockSpec(memory_space=pltpu.SMEM)
-    hbm = pl.BlockSpec(memory_space=pl.ANY)
+    hbm = pl.BlockSpec(memory_space=pltpu.HBM)
+    anywhere = pl.BlockSpec(memory_space=pl.ANY)
     vmem = pl.BlockSpec(memory_space=pltpu.VMEM)
     vector = (fields, planes, height, lanes)
     krylov, sums = pl.pallas_call(
@@ -385,21 +379,23 @@
             jax.ShapeDtypeStruct((STEPS,) + vector, f32),
             jax.ShapeDtypeStruct((1, lanes), f32),
         ),
-        in_specs=[smem, smem, hbm, hbm, hbm, hbm],
-        out_specs=(hbm, vmem),
+        in_specs=[hbm] * 6,
+        out_specs=(anywhere, vmem),
         scratch_shapes=[
             pltpu.VMEM((fields + 3, deep, height, lanes), f32),
-            pltpu.VMEM((STEPS, fields, deep, height, lanes), f32),
+            [pltpu.VMEM((fields, deep, height, lanes), f32)] * STEPS,
             pltpu.VMEM((m,) + vector, f32),
             pltpu.VMEM((fields + 3, height, lanes), f32),
             pltpu.VMEM((links - 2, fields + 3, height, lanes), f32),
-            pltpu.VMEM((STEPS, fields, 2, height, lanes), f32),
+            [pltpu.VMEM((fields, 2, height, lanes), f32)] * STEPS,
             pltpu.VMEM((4, deep, height, lanes), f32),
             pltpu.VMEM((5, 2, height, lanes), f32),
             pltpu.VMEM((count, height, lanes), f32),
             pltpu.VMEM((padded, lanes), f32),
             pltpu.VMEM((n, 1, lanes), f32),
-            pltpu.SemaphoreType.DMA((m + 3,)),
+            pltpu.SMEM(coeffs.shape, f32),
+            pltpu.SMEM(mixing_matrix.shape, f32),
+            pltpu.SemaphoreType.DMA((m + 5,)),
             pltpu.SemaphoreType.DMA((STEPS,)),
             pltpu.SemaphoreType.DMA((links,)),
             pltpu.SemaphoreType.DMA((links,)),
@@ -410,7 +406,10 @@
             collective_id=0, has_side_effects=True, vmem_limit_bytes=24 * 2**20
         ),
         name="krylov",
-    )(coeffs, mixing_matrix, basis, base_speed, span_speed, polymer_gain)
+    )(*(
+        pltpu.with_memory_space_constraint(x, pltpu.HBM)
+        for x in (coeffs, mixing_matrix, basis, base_speed, span_speed, polymer_gain)
+    ))
     chunks = 5 if fields % 5 == 0 else 1
     return pl.pallas_call(
         functools.partial(finish_kernel, float(m and basis[0].size * n), chunks),
@@ -419,14 +418,10 @@
             jax.ShapeDtypeStruct((STEPS, STEPS), f32),
             jax.ShapeDtypeStruct((STEPS,) + vector, f32),
         ),
-        in_specs=[vmem, hbm, hbm],
+        in_specs=[vmem, vmem, vmem],
         out_specs=(vmem, vmem, hbm),
         scratch_shapes=[
-            pltpu.VMEM((m,) + vector, f32),
             pltpu.VMEM((STEPS,) + vector, f32),
-            pltpu.VMEM((STEPS,) + vector, f32),
-            pltpu.SemaphoreType.DMA((chunks,)),
-            pltpu.SemaphoreType.DMA((chunks,)),
             pltpu.SemaphoreType.DMA((chunks,)),
         ],
         compiler_params=pltpu.CompilerParams(vmem_limit_bytes=24 * 2**20),

time: 35.8 us -> 27.9 us (0.78)
  local copies, waits for them, and re-layouts: 4.94 us -> 0.01 us
  Pallas kernels: 29.7 us -> 27.1 us
    unnamed x14 -> x2, local copies, waits for them, and re-layouts: 4.94 us -> 0.01 us
    pallas_call x1, Pallas kernels: 27.4 us -> 25 us  [on_device(): pl.pallas_call(functools.partial(krylov_kernel, streams, spans), out_shap...]
where the time goes in v2:
time: 27.9 us; the launch traced here: 27.7 us
  Pallas kernels  27.1 us (97%)
  between operations  0.66 us (2%)
    pallas_call x1, Pallas kernels, on_device(): pl.pallas_call(functools.partial(krylov_kernel, streams, spans), out_shap...  25 us
    pallas_call x1, Pallas kernels, on_device(): pl.pallas_call(functools.partial(finish_kernel, float(m and basis[0].size...  2.09 us

profile of v2, /device:TPU:0, one launch (start us, length us, event | category | flops | bytes accessed | tf_op | source)
XLA Modules:
  0.0 27.7 jit_solution(7837891145174789695)
XLA Ops:
  0.6 0.0 copy-start
  0.6 25.0 %krylov.1 = (f32[4,10,8,8,128]{4,3,2,1,0:T(8,128)S(1)}, f32[1,128]{1,0:T(1,128)S(1)}) custom-call(f32[4]{0:T(128)} %coeffs_in.1, f32[10,10]{1,0:T(8,128)} %mix_in.1, f32[4,10,8,8,128]{4,3,2,1,0:T(8,128)} %basis.3, f32[8,8,128]{2,1,0:T(8,128)} %base.1, f32[8,8,128]{2,1,0:T(8,128)} %span_speed.1, f32[8,8,128]{2,1,0:T(8,128)} %gain.1), custom_call_target="tpu_custom_call" | custom-call | tf_op jit(solution)/shard_map/krylov/pallas_call | solution.py:376
  25.6 0.0 copy-done
  25.6 2.1 %finish.1 = (f32[4,4]{1,0:T(4,128)}, f32[4,4]{1,0:T(4,128)}, f32[4,10,8,8,128]{4,3,2,1,0:T(8,128)}) custom-call(f32[1,128]{1,0:T(1,128)S(1)} %get-tuple-element.5.sums, f32[4,10,8,8,128]{4,3,2,1,0:T(8,128)S(1)} %copy-done, f32[4,10,8,8,128]{4,3,2,1,0:T(8,128)S(1)} %get-tuple-element.6.krylov), custom_call_target="tpu_custom_call" | custom-call | tf_op jit(solution)/shard_map/finish/pallas_call | solution.py:414
Async XLA Ops:
  0.6 25.0 %copy-start = (f32[4,10,8,8,128]{4,3,2,1,0:T(8,128)S(1)}, f32[4,10,8,8,128]{4,3,2,1,0:T(8,128)}, u32[]{:S(2)}) copy-start(f32[4,10,8,8,128]{4,3,2,1,0:T(8,128)} %basis.3) | copy-start | bytes 3932164

commit v3 on v2

--- a/solution.py
+++ b/solution.py
@@ -32,32 +32,38 @@
     ]
 
 
+def near_and_far(streams):
+    near = 4 if streams % 4 == 0 else 1
+    return near, streams // near
+
+
 def krylov_kernel(
     streams, spans,
     coeffs_in, mix_in, basis, base, span_speed, gain,
     krylov_out, sums_out,
-    ext, states, held, pack, packs, strips, coef, strip_coef, acc, rows, gathered, coeffs, mix,
+    ext, states, held, pack, packs, strips, coef, strip_coef, acc, rows, near_rows, far_rows, coeffs, mix,
     in_sem, out_sem, send_sem, recv_sem, row_send, row_recv,
 ):
     m, fields, planes = basis.shape[0], basis.shape[1], basis.shape[2]
     steps = STEPS
     lanes = basis.shape[4]
-    n = streams * spans
-    all_fields = fields + 3
     sx, sz = lax.axis_index("stream"), lax.axis_index("span")
-    me = sx * spans + sz
+    near, far = near_and_far(streams)
+    near_group = near * spans
+    place = lax.rem(sx, near)
+    near_index, far_index = place * spans + sz, sx // near
+
+    def near_device(d):
+        other = lax.rem(near_index + d, near_group)
+        return (sx - place + other // spans, lax.rem(other, spans))
+
+    def far_device(d):
+        return (lax.rem(far_index + d, far) * near + place, sz)
 
     def device(dx, dz):
         return (lax.rem(sx + dx + streams, streams), lax.rem(sz + dz + spans, spans))
 
     barrier = pltpu.get_barrier_semaphore()
-
-    def greet(d, carry):
-        other = lax.rem(me + d, n)
-        pl.semaphore_signal(
-            barrier, inc=1, device_id=(other // spans, lax.rem(other, spans)), device_id_type=MESH
-        )
-        return carry
 
     own = pl.ds(DEEP, planes)
     loads = [
@@ -71,7 +77,12 @@
     ]
     for load in loads:
         load.start()
-    lax.fori_loop(1, n, greet, 0)
+    slots = partners(spans)
+    greeted = [near_device(d) for d in range(1, near_group)]
+    greeted += [far_device(d) for d in range(1, far)]
+    greeted += [device(dx, dz) for dx, dz in slots]
+    for other in greeted:
+        pl.semaphore_signal(barrier, inc=1, device_id=other, device_id_type=MESH)
 
     lane = lax.broadcasted_iota(jnp.int32, (8, lanes), 1)
     row = lax.broadcasted_iota(jnp.int32, (8, lanes), 0)
@@ -100,7 +111,7 @@
     for i in range(3):
         packed(fields + i, [ext[fields + i, DEEP + x] for x in range(planes)])
 
-    pl.semaphore_wait(barrier, n - 1)
+    pl.semaphore_wait(barrier, len(greeted))
 
     sends = []
 
@@ -115,7 +126,6 @@
 
     send(ext.at[:, pl.ds(planes, DEEP)], ext.at[:, pl.ds(0, DEEP)], 1, 0)
     send(ext.at[:, pl.ds(DEEP, DEEP)], ext.at[:, pl.ds(planes + DEEP, DEEP)], -1, 0)
-    slots = partners(spans)
     for i, (dx, dz) in enumerate(slots):
         send(pack, packs.at[i], -dx, -dz)
 
@@ -197,6 +207,8 @@
             ]
             for x in range(lo, hi):
                 vs = [read(k, g, x) for g in range(fields)]
+                c0, c1, c2, c3 = (coef[i, x] for i in range(4))
+                gain_here = ext[fields + 2, x]
                 for f, weight, edge in zip(pair, weights, edges):
                     mixed = total(a * v for a, v in zip(weight, vs))
                     v = read(k, f, x)
@@ -204,10 +216,10 @@
                     ahead = jnp.where(lane == lanes - 1, rim, pltpu.roll(v, lanes - 1, 1))
                     behind = jnp.where(lane == 0, rim, pltpu.roll(v, 1, 1))
                     states[k][f, x] = (
-                        (coef[0, x] * read(k, f, x + 1) + coef[1, x] * read(k, f, x - 1))
-                        + (coef[2, x] * ahead + coef[3, x] * behind)
+                        (c0 * read(k, f, x + 1) + c1 * read(k, f, x - 1))
+                        + (c2 * ahead + c3 * behind)
                         + (0.05 * walls(v) - 0.3 * v)
-                        + ext[fields + 2, x] * mixed
+                        + gain_here * mixed
                     )
             if k < steps - 1:
                 for s in range(2):
@@ -250,28 +262,32 @@
     sums = jnp.sum(rows[...], axis=1, keepdims=True)
     at = lax.broadcasted_iota(jnp.int32, rows.shape, 0)
     spot = lax.broadcasted_iota(jnp.int32, rows.shape, 1)
-    gathered[me] = jnp.sum(jnp.where(at == spot, sums, 0.0), axis=0, keepdims=True)
-
-    def row_copy(d):
-        other = lax.rem(me + d, n)
-        return pltpu.make_async_remote_copy(
-            src_ref=gathered.at[me], dst_ref=gathered.at[me], send_sem=row_send, recv_sem=row_recv,
-            device_id=(other // spans, lax.rem(other, spans)), device_id_type=MESH,
+    local = jnp.sum(jnp.where(at == spot, sums, 0.0), axis=0, keepdims=True)
+
+    def summed(value, gathered, index, size, other, i):
+        if size == 1:
+            return value
+        gathered[index] = value
+        for d in range(1, size):
+            pltpu.make_async_remote_copy(
+                src_ref=gathered.at[index], dst_ref=gathered.at[index],
+                send_sem=row_send.at[i], recv_sem=row_recv.at[i],
+                device_id=other(d), device_id_type=MESH,
+            ).start()
+        others = gathered.at[pl.ds(0, size - 1)]
+        everyone = pltpu.make_async_remote_copy(
+            src_ref=others, dst_ref=others, send_sem=row_send.at[i], recv_sem=row_recv.at[i],
+            device_id=other(1), device_id_type=MESH,
         )
-
-    def share(d, carry):
-        row_copy(d).start()
-        return carry
-
-    lax.fori_loop(1, n, share, 0)
-    others = gathered.at[pl.ds(0, n - 1)]
-    everyone = pltpu.make_async_remote_copy(
-        src_ref=others, dst_ref=others, send_sem=row_send, recv_sem=row_recv,
-        device_id=device(1, 0), device_id_type=MESH,
-    )
-    everyone.wait_recv()
-    sums_out[...] = jnp.sum(gathered[...], axis=0)
-    everyone.wait_send()
+        everyone.wait_recv()
+        rows_sent.append(everyone)
+        return jnp.sum(gathered[...], axis=0)
+
+    rows_sent = []
+    close = summed(local, near_rows, near_index, near_group, near_device, 0)
+    sums_out[...] = summed(close, far_rows, far_index, far, far_device, 1)
+    for copy in rows_sent:
+        copy.wait_send()
     for copy in sends:
         copy.wait_send()
     for write in writes:
@@ -364,6 +380,7 @@
 def on_device(streams, spans, basis, coeffs, mixing_matrix, base_speed, span_speed, polymer_gain):
     m, fields, planes, height, lanes = basis.shape
     n = streams * spans
+    near, far = near_and_far(streams)
     f32 = jnp.float32
     deep = planes + 2 * DEEP
     count = m * STEPS + STEPS * (STEPS + 1) // 2 + m * (m + 1) // 2
@@ -392,15 +409,16 @@
             pltpu.VMEM((5, 2, height, lanes), f32),
             pltpu.VMEM((count, height, lanes), f32),
             pltpu.VMEM((padded, lanes), f32),
-            pltpu.VMEM((n, 1, lanes), f32),
+            pltpu.VMEM((near * spans, 1, lanes), f32),
+            pltpu.VMEM((far, 1, lanes), f32),
             pltpu.SMEM(coeffs.shape, f32),
             pltpu.SMEM(mixing_matrix.shape, f32),
             pltpu.SemaphoreType.DMA((m + 5,)),
             pltpu.SemaphoreType.DMA((STEPS,)),
             pltpu.SemaphoreType.DMA((links,)),
             pltpu.SemaphoreType.DMA((links,)),
-            pltpu.SemaphoreType.DMA,
-            pltpu.SemaphoreType.DMA,
+            pltpu.SemaphoreType.DMA((2,)),
+            pltpu.SemaphoreType.DMA((2,)),
         ],
         compiler_params=pltpu.CompilerParams(
             collective_id=0, has_side_effects=True, vmem_limit_bytes=24 * 2**20

time: 27.9 us -> 29.6 us (1.061)
  Pallas kernels: 27.1 us -> 28.7 us
    pallas_call x1, Pallas kernels: 25 us -> 26.7 us  [on_device(): pl.pallas_call(functools.partial(krylov_kernel, streams, spans), out_shap...]
where the time goes in v3:
time: 29.6 us; the launch traced here: 29.4 us
  Pallas kernels  28.7 us (97%)
  between operations  0.66 us (2%)
    pallas_call x1, Pallas kernels, on_device(): pl.pallas_call(functools.partial(krylov_kernel, streams, spans), out_shap...  26.7 us
    pallas_call x1, Pallas kernels, on_device(): pl.pallas_call(functools.partial(finish_kernel, float(m and basis[0].size...  2.09 us

profile of v3, /device:TPU:0, one launch (start us, length us, event | category | flops | bytes accessed | tf_op | source)
XLA Modules:
  0.0 29.4 jit_solution(3620265075982638115)
XLA Ops:
  0.6 0.0 copy-start
  0.6 26.7 %krylov.1 = (f32[4,10,8,8,128]{4,3,2,1,0:T(8,128)S(1)}, f32[1,128]{1,0:T(1,128)S(1)}) custom-call(f32[4]{0:T(128)} %coeffs_in.1, f32[10,10]{1,0:T(8,128)} %mix_in.1, f32[4,10,8,8,128]{4,3,2,1,0:T(8,128)} %basis.3, f32[8,8,128]{2,1,0:T(8,128)} %base.1, f32[8,8,128]{2,1,0:T(8,128)} %span_speed.1, f32[8,8,128]{2,1,0:T(8,128)} %gain.1), custom_call_target="tpu_custom_call" | custom-call | tf_op jit(solution)/shard_map/krylov/pallas_call | solution.py:393
  27.3 0.0 copy-done
  27.3 2.1 %finish.1 = (f32[4,4]{1,0:T(4,128)}, f32[4,4]{1,0:T(4,128)}, f32[4,10,8,8,128]{4,3,2,1,0:T(8,128)}) custom-call(f32[1,128]{1,0:T(1,128)S(1)} %get-tuple-element.5.sums, f32[4,10,8,8,128]{4,3,2,1,0:T(8,128)S(1)} %copy-done, f32[4,10,8,8,128]{4,3,2,1,0:T(8,128)S(1)} %get-tuple-element.6.krylov), custom_call_target="tpu_custom_call" | custom-call | tf_op jit(solution)/shard_map/finish/pallas_call | solution.py:432
Async XLA Ops:
  0.6 26.7 %copy-start = (f32[4,10,8,8,128]{4,3,2,1,0:T(8,128)S(1)}, f32[4,10,8,8,128]{4,3,2,1,0:T(8,128)}, u32[]{:S(2)}) copy-start(f32[4,10,8,8,128]{4,3,2,1,0:T(8,128)} %basis.3) | copy-start | bytes 3932164

commit v4 on v3

--- a/solution.py
+++ b/solution.py
@@ -33,7 +33,7 @@
 
 
 def near_and_far(streams):
-    near = 4 if streams % 4 == 0 else 1
+    near = 16 if streams % 16 == 0 else 1
     return near, streams // near
 
 
@@ -41,8 +41,8 @@
     streams, spans,
     coeffs_in, mix_in, basis, base, span_speed, gain,
     krylov_out, sums_out,
-    ext, states, held, pack, packs, strips, coef, strip_coef, acc, rows, near_rows, far_rows, coeffs, mix,
-    in_sem, out_sem, send_sem, recv_sem, row_send, row_recv,
+    ext, states, held, pack, packs, edge, edges_in, strips, rim_rows, coef, strip_coef, acc, rows, near_rows, far_rows, coeffs, mix,
+    in_sem, out_sem, send_sem, recv_sem, plane_send, plane_recv, row_send, row_recv,
 ):
     m, fields, planes = basis.shape[0], basis.shape[1], basis.shape[2]
     steps = STEPS
@@ -80,7 +80,8 @@
     slots = partners(spans)
     greeted = [near_device(d) for d in range(1, near_group)]
     greeted += [far_device(d) for d in range(1, far)]
-    greeted += [device(dx, dz) for dx, dz in slots]
+    if far > 1:
+        greeted += [device(dx, dz) for dx, dz in slots]
     for other in greeted:
         pl.semaphore_signal(barrier, inc=1, device_id=other, device_id_type=MESH)
 
@@ -95,25 +96,7 @@
             out = jnp.where((lane >= at) & (lane < at + WIDE), moved, out)
         pack[field] = out
 
-    for load in loads:
-        load.wait()
-
-    weights = [coeffs[j] for j in range(m)]
-
-    def start_field(f, carry):
-        values = [total(weights[j] * held[j, f, x] for j in range(m)) for x in range(planes)]
-        for x in range(planes):
-            ext[f, DEEP + x] = values[x]
-        packed(f, values)
-        return carry
-
-    lax.fori_loop(0, fields, start_field, 0)
-    for i in range(3):
-        packed(fields + i, [ext[fields + i, DEEP + x] for x in range(planes)])
-
-    pl.semaphore_wait(barrier, len(greeted))
-
-    sends = []
+    sends, plane_sends = [], []
 
     def send(src, dst, dx, dz):
         i = len(sends)
@@ -123,11 +106,61 @@
         )
         copy.start()
         sends.append(copy)
-
-    send(ext.at[:, pl.ds(planes, DEEP)], ext.at[:, pl.ds(0, DEEP)], 1, 0)
-    send(ext.at[:, pl.ds(DEEP, DEEP)], ext.at[:, pl.ds(planes + DEEP, DEEP)], -1, 0)
+        return copy
+
+    for load in loads[m:]:
+        load.wait()
+    pl.semaphore_wait(barrier, len(greeted))
+    third = pl.ds(fields, 3)
+    send(ext.at[third, pl.ds(planes + 1, DEEP - 1)], ext.at[third, pl.ds(1, DEEP - 1)], 1, 0)
+    send(ext.at[third, pl.ds(DEEP, DEEP - 1)], ext.at[third, pl.ds(planes + DEEP, DEEP - 1)], -1, 0)
+    for i in range(3):
+        packed(fields + i, [ext[fields + i, DEEP + x] for x in range(planes)])
+    for load in loads[:m]:
+        load.wait()
+    weights = [coeffs[j] for j in range(m)]
+
+    def start_field(f, carry):
+        values = [total(weights[j] * held[j, f, x] for j in range(m)) for x in range(planes)]
+        for x in range(planes):
+            ext[f, DEEP + x] = values[x]
+        packed(f, values)
+        return carry
+
+    lax.fori_loop(0, fields, start_field, 0)
+
+    half = DEEP * WIDE
+    per = lanes // half
+    tops = planes * WIDE
+    for e, begin in enumerate((half, tops)):
+        for t in range(edge.shape[1]):
+            out = jnp.zeros((8, lanes), jnp.float32)
+            for j in range(per):
+                f = t * per + j
+                if f < fields + 3:
+                    moved = pltpu.roll(pack[f], (j * half - begin) % lanes, 1)
+                    out = jnp.where((lane >= j * half) & (lane < (j + 1) * half), moved, out)
+            edge[e, t] = out
     for i, (dx, dz) in enumerate(slots):
-        send(pack, packs.at[i], -dx, -dz)
+        if dx == 0:
+            send(pack, packs.at[i - 2], -dx, -dz)
+    corner = [slot for slot in slots if slot[0] != 0]
+    for i, (dx, dz) in enumerate(corner):
+        send(edge.at[1 if dx == -1 else 0], edges_in.at[i], -dx, -dz)
+    main = pl.ds(0, fields)
+    for d in range(DEEP):
+        pair = []
+        for side, (src, dst) in enumerate((
+            (planes + DEEP - 1 - d, DEEP - 1 - d), (DEEP + d, planes + DEEP + d)
+        )):
+            copy = pltpu.make_async_remote_copy(
+                src_ref=ext.at[main, src], dst_ref=ext.at[main, dst],
+                send_sem=plane_send.at[2 * d + side], recv_sem=plane_recv.at[2 * d + side],
+                device_id=device(1 - 2 * side, 0), device_id_type=MESH,
+            )
+            copy.start()
+            pair.append(copy)
+        plane_sends.append(pair)
 
     upper = [(i, j) for i in range(m) for j in range(i, m)]
     krylov_pairs = [(k, l) for k in range(steps) for l in range(k, steps)]
@@ -156,17 +189,19 @@
         for i, value in enumerate(cooked(ext[fields, x], ext[fields + 1, x])):
             coef[i, x] = value
 
-    half = DEEP * WIDE
     inside = (lane >= half) & (lane < half + planes * WIDE)
     left_part = lane % WIDE < DEEP
 
     def strip_pair(f):
+        tile, spot = f // per, f % per
+
         def whole(dz):
-            here = pack[f] if dz == 0 else packs[slots.index((0, dz)), f]
-            before = packs[slots.index((-1, dz)), f]
-            after = packs[slots.index((1, dz)), f]
-            beside = jnp.where(lane < lanes // 2, after, before)
-            return jnp.where(inside, here, pltpu.roll(beside, lanes // 2, 1))
+            here = pack[f] if dz == 0 else packs[slots.index((0, dz)) - 2, f]
+            before = edges_in[corner.index((-1, dz)), tile]
+            after = edges_in[corner.index((1, dz)), tile]
+            before = pltpu.roll(before, (-spot * half) % lanes, 1)
+            after = pltpu.roll(after, (tops + half - spot * half) % lanes, 1)
+            return jnp.where(inside, here, jnp.where(lane < half, before, after))
 
         mine = whole(0)
         dzs = span_offsets(spans)
@@ -174,12 +209,9 @@
         right = left if len(dzs) < 2 else whole(dzs[1])
         return jnp.where(left_part, left, mine), jnp.where(left_part, mine, right)
 
-    def build_strips(f, carry):
+    for f in range(fields):
         for s, value in enumerate(strip_pair(f)):
             strips[0][f, s] = value
-        return carry
-
-    lax.fori_loop(0, fields, build_strips, 0)
     us, ws, gs = (strip_pair(fields + i) for i in range(3))
     for s in range(2):
         for i, value in enumerate(cooked(us[s], ws[s]) + (gs[s],)):
@@ -193,26 +225,50 @@
     def read(k, f, x):
         return ext[f, x] if k == 0 else states[k - 1][f, x]
 
-    writes = []
-    for k in range(steps):
-        lo, hi = 1 + k, planes + 2 * DEEP - 1 - k
-
-        def field_pair(h, carry, k=k, lo=lo, hi=hi):
-            pair = [2 * h, 2 * h + 1]
-            weights = [[mix[f, g] for g in range(fields)] for f in pair]
-            edges = [
-                jnp.where(lane % WIDE == DEEP - 1, strips[k][f, 0],
-                          pltpu.roll(strips[k][f, 1], lanes - 2, 1))
-                for f in pair
-            ]
-            for x in range(lo, hi):
+    def strip_step(k):
+        def field(f, carry):
+            weight = [mix[f, g] for g in range(fields)]
+            for s in range(2):
+                mixed = total(a * strips[k][g, s] for g, a in enumerate(weight))
+                v = strips[k][f, s]
+                strips[k + 1][f, s] = (
+                    strip_coef[0, s] * pltpu.roll(v, lanes - WIDE, 1)
+                    + strip_coef[1, s] * pltpu.roll(v, WIDE, 1)
+                    + strip_coef[2, s] * pltpu.roll(v, lanes - 1, 1)
+                    + strip_coef[3, s] * pltpu.roll(v, 1, 1)
+                    + (0.05 * walls(v) - 0.3 * v)
+                    + strip_coef[4, s] * mixed
+                )
+            return carry
+
+        lax.fori_loop(0, fields, field, 0, unroll=2 if fields % 2 == 0 else 1)
+
+    def rims(k):
+        def field(f, carry):
+            rim_rows[k][f] = jnp.where(
+                lane % WIDE == DEEP - 1, strips[k][f, 0],
+                pltpu.roll(strips[k][f, 1], lanes - 2, 1),
+            )
+            return carry
+
+        lax.fori_loop(0, fields, field, 0, unroll=2 if fields % 2 == 0 else 1)
+
+    def advance(k, which, group):
+        if not which:
+            return
+
+        def field_group(h, carry):
+            some = [group * h + i for i in range(group)]
+            weights = [[mix[f, g] for g in range(fields)] for f in some]
+            sides = [rim_rows[k][f] for f in some]
+            for x in which:
                 vs = [read(k, g, x) for g in range(fields)]
                 c0, c1, c2, c3 = (coef[i, x] for i in range(4))
                 gain_here = ext[fields + 2, x]
-                for f, weight, edge in zip(pair, weights, edges):
+                for f, weight, side in zip(some, weights, sides):
                     mixed = total(a * v for a, v in zip(weight, vs))
                     v = read(k, f, x)
-                    rim = pltpu.roll(edge, (2 * lanes - (WIDE * x + DEEP - 1)) % lanes, 1)
+                    rim = pltpu.roll(side, (2 * lanes - (WIDE * x + DEEP - 1)) % lanes, 1)
                     ahead = jnp.where(lane == lanes - 1, rim, pltpu.roll(v, lanes - 1, 1))
                     behind = jnp.where(lane == 0, rim, pltpu.roll(v, 1, 1))
                     states[k][f, x] = (
@@ -221,26 +277,31 @@
                         + (0.05 * walls(v) - 0.3 * v)
                         + gain_here * mixed
                     )
-            if k < steps - 1:
-                for s in range(2):
-                    vs = [strips[k][g, s] for g in range(fields)]
-                    for f, weight in zip(pair, weights):
-                        mixed = total(a * v for a, v in zip(weight, vs))
-                        v = strips[k][f, s]
-                        strips[k + 1][f, s] = (
-                            strip_coef[0, s] * pltpu.roll(v, lanes - WIDE, 1)
-                            + strip_coef[1, s] * pltpu.roll(v, WIDE, 1)
-                            + strip_coef[2, s] * pltpu.roll(v, lanes - 1, 1)
-                            + strip_coef[3, s] * pltpu.roll(v, 1, 1)
-                            + (0.05 * walls(v) - 0.3 * v)
-                            + strip_coef[4, s] * mixed
-                        )
             return carry
 
-        lax.fori_loop(0, fields // 2, field_pair, 0)
-        write = pltpu.make_async_copy(states[k].at[:, own], krylov_out.at[k], out_sem.at[k])
-        write.start()
-        writes.append(write)
+        lax.fori_loop(0, fields // group, field_group, 0)
+
+    for k in range(steps):
+        rims(k)
+        if k < steps - 1:
+            strip_step(k)
+    pair_size = 2 if fields % 2 == 0 else 1
+    large = 5 if fields % 5 == 0 else 1
+    last = DEEP + planes
+    for k in range(steps):
+        advance(k, range(DEEP + 1 + k, last - 1 - k), pair_size)
+    writes = []
+    for d in range(1, DEEP + 1):
+        for copy in plane_sends[d - 1]:
+            copy.wait_recv()
+        for k in range(steps):
+            advance(k, sorted({DEEP + 1 + k - d, last - 2 - k + d}), large)
+            if d == DEEP:
+                write = pltpu.make_async_copy(
+                    states[k].at[:, own], krylov_out.at[k], out_sem.at[k]
+                )
+                write.start()
+                writes.append(write)
 
     def new_products(f, sums):
         for x in range(planes):
@@ -288,7 +349,7 @@
     sums_out[...] = summed(close, far_rows, far_index, far, far_device, 1)
     for copy in rows_sent:
         copy.wait_send()
-    for copy in sends:
+    for copy in sends + [copy for pair in plane_sends for copy in pair]:
         copy.wait_send()
     for write in writes:
         write.wait()
@@ -386,6 +447,9 @@
     count = m * STEPS + STEPS * (STEPS + 1) // 2 + m * (m + 1) // 2
     padded = -(-count // 8) * 8
     links = 2 + len(partners(spans))
+    spans_beside = len(span_offsets(spans))
+    corners = 2 + 2 * spans_beside
+    tiles = -(-(fields + 3) * DEEP * WIDE // lanes)
     hbm = pl.BlockSpec(memory_space=pltpu.HBM)
     anywhere = pl.BlockSpec(memory_space=pl.ANY)
     vmem = pl.BlockSpec(memory_space=pltpu.VMEM)
@@ -403,8 +467,11 @@
             [pltpu.VMEM((fields, deep, height, lanes), f32)] * STEPS,
             pltpu.VMEM((m,) + vector, f32),
             pltpu.VMEM((fields + 3, height, lanes), f32),
-            pltpu.VMEM((links - 2, fields + 3, height, lanes), f32),
+            pltpu.VMEM((max(spans_beside, 1), fields + 3, height, lanes), f32),
+            pltpu.VMEM((2, tiles, height, lanes), f32),
+            pltpu.VMEM((corners, tiles, height, lanes), f32),
             [pltpu.VMEM((fields, 2, height, lanes), f32)] * STEPS,
+            [pltpu.VMEM((fields, height, lanes), f32)] * STEPS,
             pltpu.VMEM((4, deep, height, lanes), f32),
             pltpu.VMEM((5, 2, height, lanes), f32),
             pltpu.VMEM((count, height, lanes), f32),
@@ -417,6 +484,8 @@
             pltpu.SemaphoreType.DMA((STEPS,)),
             pltpu.SemaphoreType.DMA((links,)),
             pltpu.SemaphoreType.DMA((links,)),
+            pltpu.SemaphoreType.DMA((2 * DEEP,)),
+            pltpu.SemaphoreType.DMA((2 * DEEP,)),
             pltpu.SemaphoreType.DMA((2,)),
             pltpu.SemaphoreType.DMA((2,)),
         ],

time: 29.6 us -> 28.7 us (0.970)
  Pallas kernels: 28.7 us -> 27.9 us
    pallas_call x1, Pallas kernels: 26.7 us -> 25.8 us  [on_device(): pl.pallas_call(functools.partial(krylov_kernel, streams, spans), out_shap...]
where the time goes in v4:
time: 28.7 us; the launch traced here: 28.6 us
  Pallas kernels  27.9 us (97%)
  between operations  0.66 us (2%)
    pallas_call x1, Pallas kernels, on_device(): pl.pallas_call(functools.partial(krylov_kernel, streams, spans), out_shap...  25.8 us
    pallas_call x1, Pallas kernels, on_device(): pl.pallas_call(functools.partial(finish_kernel, float(m and basis[0].size...  2.09 us

profile of v4, /device:TPU:0, one launch (start us, length us, event | category | flops | bytes accessed | tf_op | source)
XLA Modules:
  0.0 28.6 jit_solution(13235308760521450524)
XLA Ops:
  0.6 0.0 copy-start
  0.6 25.8 %krylov.1 = (f32[4,10,8,8,128]{4,3,2,1,0:T(8,128)S(1)}, f32[1,128]{1,0:T(1,128)S(1)}) custom-call(f32[4]{0:T(128)} %coeffs_in.1, f32[10,10]{1,0:T(8,128)} %mix_in.1, f32[4,10,8,8,128]{4,3,2,1,0:T(8,128)} %basis.3, f32[8,8,128]{2,1,0:T(8,128)} %base.1, f32[8,8,128]{2,1,0:T(8,128)} %span_speed.1, f32[8,8,128]{2,1,0:T(8,128)} %gain.1), custom_call_target="tpu_custom_call" | custom-call | tf_op jit(solution)/shard_map/krylov/pallas_call | solution.py:457
  26.5 0.0 copy-done
  26.5 2.1 %finish.1 = (f32[4,4]{1,0:T(4,128)}, f32[4,4]{1,0:T(4,128)}, f32[4,10,8,8,128]{4,3,2,1,0:T(8,128)}) custom-call(f32[1,128]{1,0:T(1,128)S(1)} %get-tuple-element.5.sums, f32[4,10,8,8,128]{4,3,2,1,0:T(8,128)S(1)} %copy-done, f32[4,10,8,8,128]{4,3,2,1,0:T(8,128)S(1)} %get-tuple-element.6.krylov), custom_call_target="tpu_custom_call" | custom-call | tf_op jit(solution)/shard_map/finish/pallas_call | solution.py:501
Async XLA Ops:
  0.6 25.8 %copy-start = (f32[4,10,8,8,128]{4,3,2,1,0:T(8,128)S(1)}, f32[4,10,8,8,128]{4,3,2,1,0:T(8,128)}, u32[]{:S(2)}) copy-start(f32[4,10,8,8,128]{4,3,2,1,0:T(8,128)} %basis.3) | copy-start | bytes 3932164
